TPU v7x, 32 devices: a whole 2x2x4 slice. The times are simulated.
32 devices in a mesh: groups: 2 (over y), node: 4 (over z), chip: 4 (over x, core).
Axes of the slice: x: 2, y: 2, z: 4, core: 2. Of those that a mesh axis runs over, the one named last changes fastest.
Arguments:
- tokens: bfloat16 [4096, 8192], P(('groups', 'node'), 'chip'), parts along dimension 0, may hold values from -6 to 6
- cotangent: bfloat16 [4096, 1024], P(('groups', 'node', 'chip')), parts along dimension 0, may hold values from -6 to 6
- frozen_value_weight: bfloat16 [8192, 1024], P('chip', 'node'), may hold values from -0.0625 to 0.0625
- adapter_a: bfloat16 [16, 8192, 64], P(('groups', 'node'), 'chip'), parts along dimension 0, may hold values from -0.0625 to 0.0625
- adapter_b: bfloat16 [16, 64, 1024], P(('groups', 'node'), 'chip'), parts along dimension 0, may hold values from -0.75 to 0.75
- first_a: float32 [16, 8192, 64], P(('groups', 'node'), 'chip'), parts along dimension 0, may hold values from -60 to 60
- first_b: float32 [16, 64, 1024], P(('groups', 'node'), 'chip'), parts along dimension 0, may hold values from -60 to 60
- second_a: float32 [16, 8192, 64], P(('groups', 'node'), 'chip'), parts along dimension 0, may hold values from 10 to 1000
- second_b: float32 [16, 64, 1024], P(('groups', 'node'), 'chip'), parts along dimension 0, may hold values from 10 to 1000
- token_slot: int32 [4096], P(('groups', 'node')), parts along dimension 0, may hold values from 0 to 1, as said below
- adapter_slot: int32 [16], P('groups'), parts along dimension 0, may hold values from 0 to 7, as said below
- request_list: int32 [8, 2], P(('groups', 'node')), parts along dimension 0, may hold values from 0 to 7, as said below
- request_count: int32 [8], P(('groups', 'node')), parts along dimension 0, may hold values from 1 to 2, as said below
Outputs:
- output: bfloat16 [4096, 1024], P(('groups', 'node', 'chip')), parts along dimension 0
- new_a: bfloat16 [16, 8192, 64], P(('groups', 'node'), 'chip'), parts along dimension 0
- new_b: bfloat16 [16, 64, 1024], P(('groups', 'node'), 'chip'), parts along dimension 0
- moment_a: float32 [16, 8192, 64], P(('groups', 'node'), 'chip'), parts along dimension 0
- moment_b: float32 [16, 64, 1024], P(('groups', 'node'), 'chip'), parts along dimension 0
- square_a: float32 [16, 8192, 64], P(('groups', 'node'), 'chip'), parts along dimension 0
- square_b: float32 [16, 64, 1024], P(('groups', 'node'), 'chip'), parts along dimension 0
There are 2 independent parts, one for each index of `groups`. A program takes and returns all parts, laid end to end along the dimension named above; an argument that names none is the same for every part. Nothing has to cross between parts.
Inputs may be any that keep to these rules, and one draw needn't show every extreme that they name: `token_slot`: each token's position lies in 0 to 1; tokens at or past their node's count are padding. `adapter_slot`: A permutation of 0 to 7. `request_list`: the live entries of one node's list are distinct adapters with distinct owner nodes; entries past the count repeat live entries of the same list. `request_count`: some node has the full count and some other node the least count in every draw.
All inputs are finite; a program needn't handle non-finite values.
Results may differ from a plain program's by a relative error of at most 0.0045.
Values may be sent and summed in bfloat16 or wider, within the bound.
A program may use at most 128 MiB of HBM per device.

v0:
```python
import jax
import jax.numpy as jnp
from jax import lax
from jax.sharding import PartitionSpec as P

adapter_scale = 2.0
beta_one = 0.9
beta_two = 0.999
rate = 0.001
eps_adam = 1e-08
bias_one = 1.0
bias_two = 0.632304575229036


def adam_update(param, first, second, grad):
    first_new = beta_one * first + (1.0 - beta_one) * grad
    second_new = beta_two * second + (1.0 - beta_two) * grad * grad
    update = first_new / bias_one / (jnp.sqrt(second_new / bias_two) + eps_adam)
    return ((param.astype(jnp.float32) - rate * update).astype(jnp.bfloat16), first_new, second_new)


def local(
    tokens,
    cotangent,
    frozen_value_weight,
    adapter_a,
    adapter_b,
    first_a,
    first_b,
    second_a,
    second_b,
    token_slot,
    adapter_slot,
    request_list,
    request_count,
):
    nodes = lax.axis_size("node")
    this_node = lax.axis_index("node")
    this_chip = lax.axis_index("chip")
    owned = adapter_a.shape[0]
    most = request_list.shape[1]
    rank_part = adapter_b.shape[1]
    width_out = adapter_b.shape[2]
    rows_here = tokens.shape[0]
    positions = jnp.arange(most, dtype=jnp.int32)
    owner_ids = jnp.arange(nodes, dtype=jnp.int32)
    local_ids = jnp.arange(owned, dtype=jnp.int32)
    my_rows = jnp.take(adapter_slot, request_list[0], axis=0)
    my_owner = my_rows // owned
    my_valid = positions < request_count[0]
    all_lists, all_counts = (
        lax.all_gather(request_list, "node", axis=0, tiled=True),
        lax.all_gather(request_count, "node", axis=0, tiled=True),
    )
    all_rows = jnp.take(adapter_slot, all_lists, axis=0)
    hits = (positions[None, :] < all_counts[:, None]) & (all_rows // owned == this_node)
    picks = jnp.sum(
        (hits[:, :, None] & ((all_rows % owned)[:, :, None] == local_ids[None, None, :])).astype(
            jnp.float32
        ),
        axis=1,
    )
    picks_low = picks.astype(jnp.bfloat16)
    send_a = jnp.einsum(
        "pj,jdr->pdr", picks_low, adapter_a, preferred_element_type=jnp.float32
    ).astype(jnp.bfloat16)
    send_b = jnp.einsum(
        "pj,jrv->prv", picks_low, adapter_b, preferred_element_type=jnp.float32
    ).astype(jnp.bfloat16)
    recv_a, recv_b = (
        lax.all_to_all(send_a, "node", split_axis=0, concat_axis=0, tiled=True),
        lax.all_to_all(send_b, "node", split_axis=0, concat_axis=0, tiled=True),
    )
    fetched_a = jnp.take(recv_a, my_owner, axis=0)
    fetched_b = jnp.take(recv_b, my_owner, axis=0)
    onehot = (token_slot[:, None] == positions[None, :]) & my_valid[None, :]
    onehot_f = onehot.astype(jnp.float32)
    onehot_b = onehot.astype(jnp.bfloat16)
    low_part = jnp.einsum("td,kdr->tkr", tokens, fetched_a, preferred_element_type=jnp.float32)
    low_sel = jnp.einsum("tkr,tk->tr", low_part, onehot_f, precision=lax.Precision.HIGHEST)
    low_rank = lax.psum(low_sel, "chip")
    low_bf = low_rank.astype(jnp.bfloat16)
    low_mine = lax.dynamic_slice_in_dim(low_bf, this_chip * rank_part, rank_part, 1)
    spread_rows = (onehot_b[:, :, None] * low_mine[:, None, :]).reshape(rows_here, most * rank_part)
    up_flattened = fetched_b.reshape(most * rank_part, width_out)
    frozen_output = jnp.dot(
        tokens,
        lax.all_gather(frozen_value_weight, "node", axis=1, tiled=True),
        preferred_element_type=jnp.float32,
    )
    partial_terms = frozen_output + adapter_scale * jnp.dot(
        spread_rows, up_flattened, preferred_element_type=jnp.float32
    )
    output = lax.psum_scatter(partial_terms, "chip", scatter_dimension=0, tiled=True).astype(
        jnp.bfloat16
    )
    cot_whole = lax.all_gather(cotangent, "chip", axis=0, tiled=True)
    back_part = jnp.einsum("tv,krv->tkr", cot_whole, fetched_b, preferred_element_type=jnp.float32)
    backward_selected = jnp.einsum(
        "tkr,tk->tr", back_part, onehot_f, precision=lax.Precision.HIGHEST
    )
    backward_half_width = (adapter_scale * backward_selected).astype(jnp.bfloat16)
    back_rank = lax.all_gather(backward_half_width, "chip", axis=1, tiled=True)
    spread_back = onehot_b[:, :, None] * back_rank[:, None, :]
    grad_down = jnp.einsum("td,tkr->kdr", tokens, spread_back, preferred_element_type=jnp.float32)
    up_gradient = adapter_scale * jnp.einsum(
        "tk,tv->kv", spread_rows, cot_whole, preferred_element_type=jnp.float32
    )
    up_gradient = up_gradient.reshape(most, rank_part, width_out)
    route = (my_valid[:, None] & (my_owner[:, None] == owner_ids[None, :])).astype(jnp.float32)
    send_down = jnp.einsum("ko,kdr->odr", route, grad_down, precision=lax.Precision.HIGHEST)
    send_up = jnp.einsum("ko,krv->orv", route, up_gradient, precision=lax.Precision.HIGHEST)
    recv_down, recv_up = (
        lax.all_to_all(
            send_down.astype(jnp.bfloat16), "node", split_axis=0, concat_axis=0, tiled=True
        ).astype(send_down.dtype),
        lax.all_to_all(
            send_up.astype(jnp.bfloat16), "node", split_axis=0, concat_axis=0, tiled=True
        ).astype(send_up.dtype),
    )
    total_down = jnp.einsum("pj,pdr->jdr", picks, recv_down, precision=lax.Precision.HIGHEST)
    total_up = jnp.einsum("pj,prv->jrv", picks, recv_up, precision=lax.Precision.HIGHEST)
    new_a, moment_a, square_a = adam_update(adapter_a, first_a, second_a, total_down)
    new_b, moment_b, square_b = adam_update(adapter_b, first_b, second_b, total_up)
    return (output, new_a, new_b, moment_a, moment_b, square_a, square_b)


def solution(mesh):
    return jax.shard_map(
        local,
        mesh=mesh,
        in_specs=(
            P(("groups", "node"), "chip"),
            P(("groups", "node", "chip"), None),
            P("chip", "node"),
            P(("groups", "node"), "chip", None),
            P(("groups", "node"), "chip", None),
            P(("groups", "node"), "chip", None),
            P(("groups", "node"), "chip", None),
            P(("groups", "node"), "chip", None),
            P(("groups", "node"), "chip", None),
            P(("groups", "node")),
            P("groups"),
            P(("groups", "node"), None),
            P(("groups", "node")),
        ),
        out_specs=(
            P(("groups", "node", "chip"), None),
            P(("groups", "node"), "chip", None),
            P(("groups", "node"), "chip", None),
            P(("groups", "node"), "chip", None),
            P(("groups", "node"), "chip", None),
            P(("groups", "node"), "chip", None),
            P(("groups", "node"), "chip", None),
        ),
        check_vma=False,
    )
```

profile of v0, /device:TPU:0, one launch (start us, length us, event | category | flops | bytes accessed | tf_op | source)
XLA Modules:
  0.0 198.2 jit_solution(15936396673233152868)
XLA Ops:
  7.2 0.0 all-gather.4.cloned.1.call-start
  7.3 0.7 all-gather.4.cloned.1.call-update
  8.7 1.2 dynamic-slice
  9.9 0.8 dynamic-update-slice
  10.7 12.7 %all-gather = s32[4,1,2]{2,1,0:T(1,128)S(1)} all-gather(s32[1,1,2]{2,1,0:T(1,128)} %bitcast.84), channel_id=1, replica_groups=mesh['groups'=2,'node'=4,'chip'=4] {'node'}, dimensions={0}, use_global_device_ids=true | all-gather | bytes 40 | tf_op jit(solution)/shard_map/all_gather | solution.py:52
  23.4 13.3 %all-reduce = s32[4]{0:T(128)S(1)} all-reduce(s32[4]{0:T(128)S(1)} %dynamic-update-slice), channel_id=1, replica_groups=mesh['groups'=2,'node'=4,'chip'=4] {'node'}, use_global_device_ids=true, to_apply=%add | all-reduce | flops 4 | bytes 32
  36.7 0.1 copy.112
  36.8 0.1 copy.113
  36.9 0.1 reshape.257
  37.0 0.6 gather_fusion.1
  37.6 0.1 reshape.256
  37.7 0.1 copy.114
  37.8 0.3 convolution_convert_fusion.3
  38.1 0.7 copy.118
  38.8 3.3 %all-to-all-start.1 = ((bf16[4,16,1024]{2,1,0:T(8,128)(2,1)}), bf16[4,16,1024]{2,1,0:T(8,128)(2,1)S(1)}, u32[]{:S(2)}, u32[]{:S(2)}) async-start(bf16[4,16,1024]{2,1,0:T(8,128)(2,1)} %copy.118), calls=%async_computation.1 | async-start | bytes 262144 | tf_op jit(solution)/shard_map/all_to_all | solution.py:72
  42.2 1.0 convolution_convert_fusion.1
  43.3 1.5 copy.116
  44.8 17.1 %all-to-all-done.1 = bf16[4,16,1024]{2,1,0:T(8,128)(2,1)S(1)} async-done(((bf16[4,16,1024]{2,1,0:T(8,128)(2,1)}), bf16[4,16,1024]{2,1,0:T(8,128)(2,1)S(1)}, u32[]{:S(2)}, u32[]{:S(2)}) %all-to-all-start.1) | async-done | bytes 131104 | tf_op jit(solution)/shard_map/all_to_all | solution.py:72
  61.9 3.5 %all-to-all-start = ((bf16[4,2048,64]{1,2,0:T(8,128)(2,1)}), bf16[4,2048,64]{1,2,0:T(8,128)(2,1)S(1)}, u32[]{:S(2)}, u32[]{:S(2)}) async-start(bf16[4,2048,64]{1,2,0:T(8,128)(2,1)} %copy.116), calls=%async_computation | async-start | bytes 2097152 | tf_op jit(solution)/shard_map/all_to_all | solution.py:71
  65.4 0.0 all-gather.6.cloned.1.call-start
  65.5 0.7 all-gather.6.cloned.1.call-update
  66.2 0.0 reduce-scatter.2.cloned.1.call-start
  66.3 0.6 gather_fusion
  67.0 0.1 fusion.33
  67.0 0.5 gather_fusion.3
  67.6 46.3 %all-to-all-done = bf16[4,2048,64]{1,2,0:T(8,128)(2,1)S(1)} async-done(((bf16[4,2048,64]{1,2,0:T(8,128)(2,1)}), bf16[4,2048,64]{1,2,0:T(8,128)(2,1)S(1)}, u32[]{:S(2)}, u32[]{:S(2)}) %all-to-all-start) | async-done | bytes 1048608 | tf_op jit(solution)/shard_map/all_to_all | solution.py:71
  113.9 1.4 gather_fusion.2
  115.3 1.9 fusion.10
  117.2 12.0 %all-reduce.2 = bf16[512,64]{0,1:T(8,128)(2,1)S(1)} all-reduce(f32[512,64]{0,1:T(8,128)S(1)} %fusion.10), channel_id=1, replica_groups=mesh['groups'=2,'node'=4,'chip'=4] {'chip'}, use_global_device_ids=true, to_apply=%region_1.2 | all-reduce | flops 32768 | bytes 196608 | tf_op jit(solution)/shard_map/psum | solution.py:81
  129.2 0.0 all-gather.4.cloned.1.call-done
  129.2 4.5 %fusion.54 = f32[512,1024]{1,0:T(8,128)S(1)} fusion(bf16[512,2048]{1,0:T(8,128)(2,1)S(1)} %copy-done, bf16[2048,1024]{1,0:T(8,128)(2,1)} %all-gather.4.cloned.1.call-done), kind=kOutput, calls=%fused_computation.100 | convolution fusion | flops 2147483648 | bytes 8388608 | tf_op jit(solution)/shard_map/dot_general | solution.py:86
  133.8 1.8 fusion
  135.6 1.6 convolution_multiply_fusion
  137.2 0.5 convolution_convert_fusion.2
  137.8 0.7 copy.126
  138.5 3.7 %all-to-all-start.3 = ((bf16[4,16,1024]{2,1,0:T(8,128)(2,1)}), bf16[4,16,1024]{2,1,0:T(8,128)(2,1)S(1)}, u32[]{:S(2)}, u32[]{:S(2)}) async-start(bf16[4,16,1024]{2,1,0:T(8,128)(2,1)} %copy.126), calls=%async_computation.4 | async-start | bytes 262144 | tf_op jit(solution)/shard_map/all_to_all | solution.py:117
  142.2 0.4 fusion.14
  142.6 5.2 %all_gather.19 = bf16[512,64]{0,1:T(8,128)(2,1)S(1)} all-gather(bf16[512,16]{0,1:T(8,128)(2,1)S(1)} %multiply_convert_fusion), channel_id=1, replica_groups=mesh['groups'=2,'node'=4,'chip'=4] {'chip'}, dimensions={1}, use_global_device_ids=true | all-gather | bytes 81920 | tf_op jit(solution)/shard_map/all_gather | solution.py:103
  147.9 0.5 convolution_bitcast_fusion
  148.3 3.1 %convolution_convert_fusion = bf16[4,2048,64]{1,0,2:T(4,128)(2,1)S(1)} fusion(f32[2,2048,64]{1,2,0:T(8,128)S(1)} %convolution_bitcast_fusion, pred[2]{0:T(512)(128)(4,1)S(1)} %iota_compare_fusion, s32[2]{0:T(128)S(1)} %get-tuple-element.42), kind=kOutput, calls=%fused_computation.4 | convolution fusion | flops 13107216 | bytes 2097162 | tf_op jit(solution)/shard_map/ko,kdr->odr/dot_general | solution.py:111
  151.4 1.5 copy.120
  153.0 5.1 %all-to-all-start.2 = ((bf16[4,2048,64]{1,2,0:T(8,128)(2,1)}), bf16[4,2048,64]{1,2,0:T(8,128)(2,1)S(1)}, u32[]{:S(2)}, u32[]{:S(2)}) async-start(bf16[4,2048,64]{1,2,0:T(8,128)(2,1)} %copy.120), calls=%async_computation.3 | async-start | bytes 2097152 | tf_op jit(solution)/shard_map/all_to_all | solution.py:114
  158.1 0.4 fusion.27
  158.5 1.7 subtract_convert_fusion.1
  160.2 24.1 %all-to-all-done.2 = bf16[4,2048,64]{1,2,0:T(8,128)(2,1)S(1)} async-done(((bf16[4,2048,64]{1,2,0:T(8,128)(2,1)}), bf16[4,2048,64]{1,2,0:T(8,128)(2,1)S(1)}, u32[]{:S(2)}, u32[]{:S(2)}) %all-to-all-start.2) | async-done | bytes 1048608 | tf_op jit(solution)/shard_map/all_to_all | solution.py:114
  184.3 2.0 %fusion.18 = f32[2,2048,64]{1,0,2:T(2,128)S(1)} fusion(bf16[4,2048,64]{1,2,0:T(8,128)(2,1)S(1)} %all-to-all-done.2, f32[4,2]{0,1:T(2,128)S(1)} %fusion.34), kind=kOutput, calls=%fused_computation.27 | convolution fusion | flops 12582912 | bytes 2097184 | tf_op jit(solution)/shard_map/pj,pdr->jdr/dot_general | solution.py:121
  186.3 3.6 %subtract_convert_fusion = (bf16[2,2048,64]{1,2,0:T(8,128)(2,1)}, f32[2,2048,64]{1,2,0:T(8,128)}, f32[2,2048,64]{1,2,0:T(8,128)}) fusion(bf16[2,2048,64]{1,2,0:T(8,128)(2,1)} %param.16, f32[2,2048,64]{1,0,2:T(2,128)S(1)} %fusion.18, f32[2,2048,64]{1,2,0:T(8,128)S(1)} %copy-done.3, f32[2,2048,64]{1,2,0:T(8,128)S(1)} %copy-done.4), kind=kLoop, calls=%fused_computation.25 | loop fusion | flops 3670016 | bytes 6291456 | tf_op jit(solution)/shard_map/convert_element_type | solution.py:19
  189.9 1.8 convert_element_type.56
  (39 shorter events, 0.3 us)
Async XLA Ops:
  7.2 108.1 %copy-start = (bf16[512,2048]{1,0:T(8,128)(2,1)S(1)}, bf16[512,2048]{1,0:T(8,128)(2,1)}, u32[]{:S(2)}) copy-start(bf16[512,2048]{1,0:T(8,128)(2,1)} %param.13) | copy-start | bytes 6291460
  7.2 29.8 %copy-start.1 = (s32[8]{0:T(128)S(1)}, s32[8]{0:T(128)}, u32[]{:S(2)}) copy-start(s32[8]{0:T(128)} %param.23) | copy-start | bytes 100
  7.2 30.6 %copy-start.7 = (bf16[2,16,1024]{2,1,0:T(8,128)(2,1)S(1)}, bf16[2,16,1024]{2,1,0:T(8,128)(2,1)}, u32[]{:S(2)}) copy-start(bf16[2,16,1024]{2,1,0:T(8,128)(2,1)} %param.17) | copy-start | bytes 196612
  7.2 35.0 %copy-start.5 = (bf16[2,2048,64]{1,2,0:T(8,128)(2,1)S(1)}, bf16[2,2048,64]{1,2,0:T(8,128)(2,1)}, u32[]{:S(2)}) copy-start(bf16[2,2048,64]{1,2,0:T(8,128)(2,1)} %param.16) | copy-start | bytes 1572868
  7.2 122.0 %all-gather.4.cloned.1.call-start = ((), (), s32[]{:S(2)}) async-start(), calls=%async_computation.5 | async-start | bytes 5242880 | tf_op jit(solution)/shard_map/all_gather | solution.py:88
  38.8 23.1 %all-to-all-start.1 = ((bf16[4,16,1024]{2,1,0:T(8,128)(2,1)}), bf16[4,16,1024]{2,1,0:T(8,128)(2,1)S(1)}, u32[]{:S(2)}, u32[]{:S(2)}) async-start(bf16[4,16,1024]{2,1,0:T(8,128)(2,1)} %copy.118), calls=%async_computation.1 | async-start | bytes 262144 | tf_op jit(solution)/shard_map/all_to_all | solution.py:72
  43.2 23.0 %copy-start.9 = (s32[1,2]{1,0:T(1,128)S(1)}, s32[1,2]{1,0:T(1,128)}, u32[]{:S(2)}) copy-start(s32[1,2]{1,0:T(1,128)} %param.24) | copy-start | bytes 28
  43.2 23.7 %copy-start.8 = (s32[512]{0:T(512)S(1)}, s32[512]{0:T(512)}, u32[]{:S(2)}) copy-start(s32[512]{0:T(512)} %param.22) | copy-start | bytes 6148
  61.9 52.0 %all-to-all-start = ((bf16[4,2048,64]{1,2,0:T(8,128)(2,1)}), bf16[4,2048,64]{1,2,0:T(8,128)(2,1)S(1)}, u32[]{:S(2)}, u32[]{:S(2)}) async-start(bf16[4,2048,64]{1,2,0:T(8,128)(2,1)} %copy.116), calls=%async_computation | async-start | bytes 2097152 | tf_op jit(solution)/shard_map/all_to_all | solution.py:71
  65.4 70.2 %all-gather.6.cloned.1.call-start = ((), (), s32[]{:S(2)}) async-start(), calls=%async_computation.7 | async-start | bytes 1310720 | tf_op jit(solution)/shard_map/all_gather | solution.py:97
  66.2 123.7 %reduce-scatter.2.cloned.1.call-start = ((), (), s32[]{:S(2)}) async-start(), calls=%async_computation.6 | async-start | bytes 2621440 | tf_op jit(solution)/shard_map/reduce_scatter | solution.py:94
  135.6 6.6 %copy-start.2 = (bf16[512,1024]{1,0:T(8,128)(2,1)S(1)}, bf16[512,1024]{1,0:T(8,128)(2,1)}, u32[]{:S(2)}) copy-start(bf16[512,1024]{1,0:T(8,128)(2,1)} %all-gather.6.cloned.1.call-done) | copy-start | bytes 3145732
  138.5 14.5 %all-to-all-start.3 = ((bf16[4,16,1024]{2,1,0:T(8,128)(2,1)}), bf16[4,16,1024]{2,1,0:T(8,128)(2,1)S(1)}, u32[]{:S(2)}, u32[]{:S(2)}) async-start(bf16[4,16,1024]{2,1,0:T(8,128)(2,1)} %copy.126), calls=%async_computation.4 | async-start | bytes 262144 | tf_op jit(solution)/shard_map/all_to_all | solution.py:117
  151.4 7.0 %copy-start.6 = (f32[2,16,1024]{2,1,0:T(8,128)S(1)}, f32[2,16,1024]{2,1,0:T(8,128)}, u32[]{:S(2)}) copy-start(f32[2,16,1024]{2,1,0:T(8,128)} %param.21) | copy-start | bytes 393220
  153.0 31.3 %all-to-all-start.2 = ((bf16[4,2048,64]{1,2,0:T(8,128)(2,1)}), bf16[4,2048,64]{1,2,0:T(8,128)(2,1)S(1)}, u32[]{:S(2)}, u32[]{:S(2)}) async-start(bf16[4,2048,64]{1,2,0:T(8,128)(2,1)} %copy.120), calls=%async_computation.3 | async-start | bytes 2097152 | tf_op jit(solution)/shard_map/all_to_all | solution.py:114
  184.3 2.0 %copy-start.3 = (f32[2,2048,64]{1,2,0:T(8,128)S(1)}, f32[2,2048,64]{1,2,0:T(8,128)}, u32[]{:S(2)}) copy-start(f32[2,2048,64]{1,2,0:T(8,128)} %param.20) | copy-start | bytes 3145732
  184.3 2.0 %copy-start.4 = (f32[2,2048,64]{1,2,0:T(8,128)S(1)}, f32[2,2048,64]{1,2,0:T(8,128)}, u32[]{:S(2)}) copy-start(f32[2,2048,64]{1,2,0:T(8,128)} %param.18) | copy-start | bytes 3145732
Sparse Core Ops, SparseCore 0:
  9.6 108.3 all-gather.3
  119.6 15.5 all-gather.5
  137.7 30.9 reduce-scatter.1
where the time goes:
time: 199 us; the launch traced here: 198 us
  waiting for transfers between devices  89 us (45%)
  blocking collectives  43.2 us (22%)
  matrix products  18 us (9%)
  starting transfers between devices  15.8 us (8%)
  between operations  14.8 us (7%)
  local copies, waits for them, and re-layouts  10.2 us (5%)
  other arithmetic  7.28 us (4%)
    all_to_all x1, waiting for transfers between devices, local(): lax.all_to_all(send_a, 'node', split_axis=0, concat_axis=0, tiled=True)  46.3 us
    all_to_all x1, waiting for transfers between devices, local(): lax.all_to_all(send_down.astype(jnp.bfloat16), 'node', split_axis=0, conc...  24.1 us
    all_to_all x1, waiting for transfers between devices, local(): lax.all_to_all(send_b, 'node', split_axis=0, concat_axis=0, tiled=True)  17.1 us
    unnamed x1, blocking collectives  13.3 us
    all_gather x1, blocking collectives, local(): lax.all_gather(request_list, 'node', axis=0, tiled=True)  12.7 us
    psum x1, blocking collectives, local(): low_rank = lax.psum(low_sel, 'chip')  12 us
    convert_element_type x2, other arithmetic, adam_update(): (param.astype(jnp.float32) - rate * update).astype(jnp.bfloat16)  5.28 us
    all_gather x1, blocking collectives, local(): back_rank = lax.all_gather(backward_half_width, 'chip', axis=1, tiled=True)  5.25 us
  transfers between devices with their start and end apart: 7, of which 3 were waited for; matrix products, arithmetic and copies ran while one was open for 17% of the time, Pallas kernels for 0%

commit v1 on v0

--- a/solution.py
+++ b/solution.py
@@ -1,6 +1,10 @@
+import functools
+
 import jax
 import jax.numpy as jnp
 from jax import lax
+from jax.experimental import pallas as pl
+from jax.experimental.pallas import tpu as pltpu
 from jax.sharding import PartitionSpec as P
 
 adapter_scale = 2.0
@@ -19,7 +23,7 @@
     return ((param.astype(jnp.float32) - rate * update).astype(jnp.bfloat16), first_new, second_new)
 
 
-def local(
+def local_plain(
     tokens,
     cotangent,
     frozen_value_weight,
@@ -125,7 +129,504 @@
     return (output, new_a, new_b, moment_a, moment_b, square_a, square_b)
 
 
+MESH = pl.DeviceIdType.MESH
+NT = (((1,), (1,)), ((), ()))
+TN = (((0,), (0,)), ((), ()))
+F32 = jnp.float32
+BF16 = jnp.bfloat16
+
+
+def rows_of(index, size):
+    return pl.ds(pl.multiple_of(index * size, size), size)
+
+
+def step_kernel(
+    nodes,
+    chips,
+    groups,
+    slot_ref,
+    list_ref,
+    count_ref,
+    token_slot_ref,
+    tokens_ref,
+    cot_ref,
+    w_ref,
+    a_ref,
+    b_ref,
+    out_ref,
+    total_a_ref,
+    total_b_ref,
+    info,
+    cot_all,
+    w_all,
+    send_a,
+    recv_a,
+    send_b,
+    recv_b,
+    back_all,
+    grad_a,
+    got_a,
+    grad_b,
+    got_b,
+    low_all,
+    low_send,
+    low_recv,
+    lora,
+    part_send,
+    part_recv,
+    info_sem,
+    cot_sem,
+    a_sem,
+    b_sem,
+    back_sem,
+    low_sem,
+    ga_sem,
+    gb_sem,
+    w_sem,
+    wg_send_sem,
+    wg_recv_sem,
+    part_send_sem,
+    part_recv_sem,
+):
+    me = lax.axis_index("node")
+    chip = lax.axis_index("chip")
+    group = lax.axis_index("groups")
+    owned, rank, depth = a_ref.shape
+    rank_part = b_ref.shape[1]
+    most = list_ref.shape[1]
+    tokens_n = tokens_ref.shape[0]
+    out_rows, width = cot_ref.shape
+    w_cols = w_ref.shape[1]
+    half = depth // groups
+
+    barrier = pltpu.get_barrier_semaphore()
+    for axis, size, here in (("node", nodes, me), ("chip", chips, chip), ("groups", groups, group)):
+        for o in range(1, size):
+            pl.semaphore_signal(
+                barrier, inc=1, device_id={axis: lax.rem(here + o, size)}, device_id_type=MESH
+            )
+
+    lane = lax.broadcasted_iota(jnp.int32, (8, 128), 1)
+    mine = jnp.full((8, 128), -1, jnp.int32)
+    slots = token_slot_ref[...]
+    tok_row = jnp.full(slots.shape, -1, jnp.int32)
+    for k in range(most):
+        row = jnp.where(k < count_ref[0], slot_ref[list_ref[0, k]], -1)
+        mine = jnp.where(lane == k, row, mine)
+        tok_row = jnp.where(slots == k, row, tok_row)
+    info[me] = mine
+    masks = [
+        jnp.where((tok_row >= p * owned) & (tok_row < (p + 1) * owned), 1.0, 0.0).astype(F32)
+        for p in range(nodes)
+    ]
+    pl.semaphore_wait(barrier, nodes + chips + groups - 3)
+
+    def exchange(axis, size, here, sem, src_of, dst):
+        copies = []
+        for o in range(1, size):
+            peer = lax.rem(here + o, size)
+            copies.append(
+                pltpu.make_async_remote_copy(
+                    src_ref=src_of(peer),
+                    dst_ref=dst,
+                    send_sem=sem.at[0, o - 1],
+                    recv_sem=sem.at[1, o - 1],
+                    device_id={axis: peer},
+                    device_id_type=MESH,
+                )
+            )
+        return copies
+
+    def start(copies):
+        for c in copies:
+            c.start()
+
+    def landed(copies):
+        for c in copies:
+            c.wait_recv()
+
+    info_copies = exchange("node", nodes, me, info_sem, lambda q: info.at[me], info.at[me])
+    start(info_copies)
+    cot_copies = exchange(
+        "chip", chips, chip, cot_sem, lambda q: cot_ref, cot_all.at[rows_of(chip, out_rows)]
+    )
+    start(cot_copies)
+
+    my_half = rows_of(group, half)
+
+    def w_hop(way, j):
+        shard = me - j if way == 0 else me + j
+        have = (shard >= 0) if way == 0 else (shard < nodes)
+        may = (me < nodes - 1) if way == 0 else (me > 0)
+        peer = me + 1 if way == 0 else me - 1
+        src = w_ref.at[my_half] if j == 0 else w_all.at[shard, my_half]
+        copy = pltpu.make_async_remote_copy(
+            src_ref=src,
+            dst_ref=w_all.at[shard, my_half],
+            send_sem=w_sem.at[0, way, j],
+            recv_sem=w_sem.at[1, way, j],
+            device_id={"node": peer},
+            device_id_type=MESH,
+        )
+        return have & may, copy
+
+    def w_from(way, j):
+        shard = me - 1 - j if way == 0 else me + 1 + j
+        have = (shard >= 0) if way == 0 else (shard < nodes)
+        return have, shard
+
+    def w_share(way, j, shard):
+        copies = []
+        for o in range(1, groups):
+            copies.append(
+                pltpu.make_async_remote_copy(
+                    src_ref=w_all.at[shard, my_half],
+                    dst_ref=w_all.at[shard, my_half],
+                    send_sem=wg_send_sem.at[way, j, o - 1],
+                    recv_sem=wg_recv_sem.at[way, j, o - 1],
+                    device_id={"groups": lax.rem(group + o, groups)},
+                    device_id_type=MESH,
+                )
+            )
+        return copies
+
+    def w_send(way, j):
+        go, copy = w_hop(way, j)
+
+        @pl.when(go)
+        def _():
+            copy.start()
+
+    def w_step(j):
+        for way in (0, 1):
+            have, shard = w_from(way, j)
+
+            @pl.when(have)
+            def _():
+                pltpu.make_async_remote_copy(
+                    src_ref=w_all.at[shard, my_half],
+                    dst_ref=w_all.at[shard, my_half],
+                    send_sem=w_sem.at[0, way, j],
+                    recv_sem=w_sem.at[1, way, j],
+                    device_id={"node": me - 1 if way == 0 else me + 1},
+                    device_id_type=MESH,
+                ).wait_recv()
+                start(w_share(way, j, shard))
+
+            if j + 1 < nodes - 1:
+                w_send(way, j + 1)
+
+    w_send(0, 0)
+    w_send(1, 0)
+    cot_all[rows_of(chip, out_rows), :] = cot_ref[...]
+
+    landed(info_copies)
+
+    def picks(q):
+        found = info[q]
+        return [
+            jnp.max(jnp.where(found == me * owned + j, 1.0, 0.0).astype(F32)) for j in range(owned)
+        ]
+
+    b_copies = exchange(
+        "node",
+        nodes,
+        me,
+        b_sem,
+        lambda q: send_b.at[rows_of(q, rank_part)],
+        recv_b.at[rows_of(me, rank_part)],
+    )
+    a_copies = exchange(
+        "node", nodes, me, a_sem, lambda q: send_a.at[rows_of(q, rank)], recv_a.at[rows_of(me, rank)]
+    )
+    for o in range(1, nodes + 1):
+        q = lax.rem(me + o, nodes)
+        pick = picks(q)
+        chosen = sum(pick[j] * b_ref[j].astype(F32) for j in range(owned)).astype(BF16)
+        if o < nodes:
+            send_b[rows_of(q, rank_part), :] = chosen
+            b_copies[o - 1].start()
+        else:
+            recv_b[rows_of(me, rank_part), :] = chosen
+    for o in range(1, nodes + 1):
+        q = lax.rem(me + o, nodes)
+        pick = picks(q)
+        chosen = sum(pick[j] * a_ref[j].astype(F32) for j in range(owned)).astype(BF16)
+        if o < nodes:
+            send_a[rows_of(q, rank), :] = chosen
+            a_copies[o - 1].start()
+        else:
+            recv_a[rows_of(me, rank), :] = chosen
+
+    landed(cot_copies)
+    landed(b_copies)
+    every = lax.dot_general(recv_b[...], cot_all[...], NT, preferred_element_type=F32)
+    back = sum(
+        masks[p] * every[p * rank_part : (p + 1) * rank_part] for p in range(nodes)
+    )
+    back_all[rows_of(chip, rank_part), :] = (adapter_scale * back).astype(BF16)
+    back_copies = exchange(
+        "chip",
+        chips,
+        chip,
+        back_sem,
+        lambda q: back_all.at[rows_of(chip, rank_part)],
+        back_all.at[rows_of(chip, rank_part)],
+    )
+    start(back_copies)
+    w_step(0)
+    landed(back_copies)
+
+    whole_back = back_all[...].astype(F32)
+    spread_back = jnp.concatenate([masks[p] * whole_back for p in range(nodes)], axis=0).astype(BF16)
+    tile = min(512, depth)
+    for t in range(depth // tile):
+        cols = slice(t * tile, (t + 1) * tile)
+        grad_a[:, cols] = jnp.dot(
+            spread_back, tokens_ref[:, cols], preferred_element_type=F32
+        ).astype(BF16)
+    ga_copies = exchange(
+        "node", nodes, me, ga_sem, lambda q: grad_a.at[rows_of(q, rank)], got_a.at[rows_of(me, rank)]
+    )
+    start(ga_copies)
+    got_a[rows_of(me, rank), :] = grad_a[rows_of(me, rank), :]
+
+    if nodes > 2:
+        w_step(1)
+
+    landed(a_copies)
+    low_all[...] = lax.dot_general(
+        recv_a[...], tokens_ref[...], NT, preferred_element_type=F32
+    )
+    low_send[...] = sum(masks[p] * low_all[p * rank : (p + 1) * rank, :] for p in range(nodes))
+    low_copies = exchange(
+        "chip",
+        chips,
+        chip,
+        low_sem,
+        lambda q: low_send.at[rows_of(q, rank_part)],
+        low_recv.at[chip],
+    )
+    start(low_copies)
+    low_recv[chip] = low_send[rows_of(chip, rank_part), :]
+    landed(low_copies)
+    low_mine = sum(low_recv[c] for c in range(chips)).astype(BF16).astype(F32)
+    spread_low = jnp.concatenate([masks[p] * low_mine for p in range(nodes)], axis=0).astype(BF16)
+    grad_b[...] = (
+        adapter_scale * jnp.dot(spread_low, cot_all[...], preferred_element_type=F32)
+    ).astype(BF16)
+    gb_copies = exchange(
+        "node",
+        nodes,
+        me,
+        gb_sem,
+        lambda q: grad_b.at[rows_of(q, rank_part)],
+        got_b.at[rows_of(me, rank_part)],
+    )
+    start(gb_copies)
+    got_b[rows_of(me, rank_part), :] = grad_b[rows_of(me, rank_part), :]
+    lora[...] = adapter_scale * lax.dot_general(
+        spread_low, recv_b[...], TN, preferred_element_type=F32
+    )
+
+    def part_copies(shard):
+        copies = []
+        cols = rows_of(shard, w_cols)
+        for o in range(1, chips):
+            peer = lax.rem(chip + o, chips)
+            copies.append(
+                pltpu.make_async_remote_copy(
+                    src_ref=part_send.at[rows_of(peer, out_rows), cols],
+                    dst_ref=part_recv.at[chip, :, cols],
+                    send_sem=part_send_sem.at[shard, o - 1],
+                    recv_sem=part_recv_sem.at[shard, o - 1],
+                    device_id={"chip": peer},
+                    device_id_type=MESH,
+                )
+            )
+        return copies
+
+    def chunk(shard, weight):
+        cols = rows_of(shard, w_cols)
+
+        def body(c, carry):
+            rows = rows_of(c, out_rows)
+            part_send[rows, cols] = (
+                jnp.dot(tokens_ref[rows, :], weight[...], preferred_element_type=F32)
+                + lora[rows, cols]
+            ).astype(BF16)
+            return carry
+
+        lax.fori_loop(0, chips, body, 0)
+        start(part_copies(shard))
+
+    chunk(me, w_ref)
+    for j in range(nodes - 1):
+        if j >= 2:
+            w_step(j)
+        for way in (0, 1):
+            have, shard = w_from(way, j)
+
+            @pl.when(have)
+            def _():
+                for o in range(1, groups):
+                    theirs = rows_of(lax.rem(group + groups - o, groups), half)
+                    pltpu.make_async_remote_copy(
+                        src_ref=w_all.at[shard, theirs],
+                        dst_ref=w_all.at[shard, theirs],
+                        send_sem=wg_send_sem.at[way, j, o - 1],
+                        recv_sem=wg_recv_sem.at[way, j, o - 1],
+                        device_id={"groups": lax.rem(group + o, groups)},
+                        device_id_type=MESH,
+                    ).wait_recv()
+                chunk(shard, w_all.at[shard])
+
+    landed(ga_copies)
+    landed(gb_copies)
+    weights = [picks(q) for q in range(nodes)]
+    for j in range(owned):
+        total_a_ref[j] = sum(
+            weights[q][j] * got_a[q * rank : (q + 1) * rank, :].astype(F32) for q in range(nodes)
+        )
+        total_b_ref[j] = sum(
+            weights[q][j] * got_b[q * rank_part : (q + 1) * rank_part, :].astype(F32)
+            for q in range(nodes)
+        )
+
+    for shard in range(nodes):
+        landed(part_copies(shard))
+    part_recv[chip] = part_send[rows_of(chip, out_rows), :]
+    out_ref[...] = sum(part_recv[c].astype(F32) for c in range(chips)).astype(BF16)
+
+    for copies in (
+        info_copies,
+        cot_copies,
+        b_copies,
+        a_copies,
+        back_copies,
+        ga_copies,
+        low_copies,
+        gb_copies,
+    ):
+        for c in copies:
+            c.wait_send()
+    for shard in range(nodes):
+        for c in part_copies(shard):
+            c.wait_send()
+    for j in range(nodes - 1):
+        for way in (0, 1):
+            go, copy = w_hop(way, j)
+
+            @pl.when(go)
+            def _():
+                copy.wait_send()
+
+            have, shard = w_from(way, j)
+
+            @pl.when(have)
+            def _():
+                for c in w_share(way, j, shard):
+                    c.wait_send()
+
+
+def local_fused(
+    nodes,
+    chips,
+    groups,
+    tokens,
+    cotangent,
+    frozen_value_weight,
+    adapter_a,
+    adapter_b,
+    first_a,
+    first_b,
+    second_a,
+    second_b,
+    token_slot,
+    adapter_slot,
+    request_list,
+    request_count,
+):
+    owned, depth, rank = adapter_a.shape
+    rank_part = adapter_b.shape[1]
+    rows = tokens.shape[0]
+    out_rows, width = cotangent.shape
+    w_cols = frozen_value_weight.shape[1]
+    vmem = pl.BlockSpec(memory_space=pltpu.VMEM)
+    smem = pl.BlockSpec(memory_space=pltpu.SMEM)
+    dma = pltpu.SemaphoreType.DMA
+    output, total_a, total_b = pl.pallas_call(
+        functools.partial(step_kernel, nodes, chips, groups),
+        out_shape=(
+            jax.ShapeDtypeStruct((out_rows, width), BF16),
+            jax.ShapeDtypeStruct((owned, rank, depth), F32),
+            jax.ShapeDtypeStruct((owned, rank_part, width), F32),
+        ),
+        in_specs=[smem] * 3 + [vmem] * 6,
+        out_specs=(vmem, vmem, vmem),
+        scratch_shapes=[
+            pltpu.VMEM((nodes, 8, 128), jnp.int32),
+            pltpu.VMEM((rows, width), BF16),
+            pltpu.VMEM((nodes, depth, w_cols), BF16),
+            pltpu.VMEM((nodes * rank, depth), BF16),
+            pltpu.VMEM((nodes * rank, depth), BF16),
+            pltpu.VMEM((nodes * rank_part, width), BF16),
+            pltpu.VMEM((nodes * rank_part, width), BF16),
+            pltpu.VMEM((rank, rows), BF16),
+            pltpu.VMEM((nodes * rank, depth), BF16),
+            pltpu.VMEM((nodes * rank, depth), BF16),
+            pltpu.VMEM((nodes * rank_part, width), BF16),
+            pltpu.VMEM((nodes * rank_part, width), BF16),
+            pltpu.VMEM((nodes * rank, rows), F32),
+            pltpu.VMEM((rank, rows), F32),
+            pltpu.VMEM((chips, rank_part, rows), F32),
+            pltpu.VMEM((rows, width), F32),
+            pltpu.VMEM((rows, width), BF16),
+            pltpu.VMEM((chips, out_rows, width), BF16),
+            dma((2, nodes - 1)),
+            dma((2, chips - 1)),
+            dma((2, nodes - 1)),
+            dma((2, nodes - 1)),
+            dma((2, chips - 1)),
+            dma((2, chips - 1)),
+            dma((2, nodes - 1)),
+            dma((2, nodes - 1)),
+            dma((2, 2, nodes - 1)),
+            dma((2, nodes - 1, groups - 1)),
+            dma((2, nodes - 1, groups - 1)),
+            dma((nodes, chips - 1)),
+            dma((nodes, chips - 1)),
+        ],
+        compiler_params=pltpu.CompilerParams(
+            collective_id=0, has_side_effects=True, vmem_limit_bytes=48 * 1024 * 1024
+        ),
+        cost_estimate=pl.CostEstimate(
+            flops=2 * rows * depth * (width + 2 * nodes * rank),
+            bytes_accessed=8 * 1024 * 1024,
+            transcendentals=0,
+        ),
+    )(
+        adapter_slot,
+        request_list,
+        request_count,
+        token_slot.reshape(1, rows),
+        tokens,
+        cotangent,
+        frozen_value_weight,
+        jnp.swapaxes(adapter_a, 1, 2),
+        adapter_b,
+    )
+    new_a, moment_a, square_a = adam_update(
+        adapter_a, first_a, second_a, jnp.swapaxes(total_a, 1, 2)
+    )
+    new_b, moment_b, square_b = adam_update(adapter_b, first_b, second_b, total_b)
+    return (output, new_a, new_b, moment_a, moment_b, square_a, square_b)
+
+
 def solution(mesh):
+    nodes, chips, groups = (mesh.shape[name] for name in ("node", "chip", "groups"))
+    fits = 2 <= nodes <= 4 and chips >= 2 and groups >= 2
+    local = functools.partial(local_fused, nodes, chips, groups) if fits else local_plain
     return jax.shard_map(
         local,
         mesh=mesh,

time: 199 us -> 117 us (0.59)
  Pallas kernels: 0 us -> 104 us
  waiting for transfers between devices: 89 us -> 0 us
  blocking collectives: 43.2 us -> 0 us
  matrix products: 18 us -> 0 us
  starting transfers between devices: 15.8 us -> 0 us
  between operations: 14.8 us -> 1.34 us
  other arithmetic: 7.28 us -> 2.76 us
    pallas_call x0 -> x1, Pallas kernels: none -> 104 us  [local_fused(): pl.pallas_call(functools.partial(step_kernel, nodes, chips, groups), out_...]
    all_to_all x4 -> x0, waiting for transfers between devices: 87.6 us -> none  [the longest x1 46.3 us: local(): lax.all_to_all(send_a, 'node', split_axis=0, concat_axis=0, tiled=True)]
    dot_general x12 -> x0, matrix products: 18 us -> none  [the longest x1 4.53 us: local(): jnp.dot(tokens, lax.all_gather(frozen_value_weight, 'node', axis=1, tiled...]
    all_gather x2 -> x0, blocking collectives: 17.9 us -> none  [the longest x1 12.7 us: local(): lax.all_gather(request_list, 'node', axis=0, tiled=True)]
    all_to_all x4 -> x0, starting transfers between devices: 15.6 us -> none  [the longest x1 5.09 us: local(): lax.all_to_all(send_down.astype(jnp.bfloat16), 'node', split_axis=0, conc...]
    unnamed x1 -> x0, blocking collectives: 13.3 us -> none
    psum x1 -> x0, blocking collectives: 12 us -> none  [local(): low_rank = lax.psum(low_sel, 'chip')]
    unnamed x23 -> x25, local copies, waits for them, and re-layouts: 2.05 us -> 8.35 us
  transfers between devices with their start and end apart: 7 -> 0, of which waited for: 3 -> 0; matrix products, arithmetic and copies ran while one was open for 17% -> 0% of each run, Pallas kernels for 0% -> 0%
where the time goes in v1:
time: 117 us
  Pallas kernels  104 us (89%)
  local copies, waits for them, and re-layouts  8.35 us (7%)
  other arithmetic  2.76 us (2%)
  between operations  1.34 us (1%)
    pallas_call x1, Pallas kernels, local_fused(): pl.pallas_call(functools.partial(step_kernel, nodes, chips, groups), out_...  104 us
    unnamed x25, local copies, waits for them, and re-layouts  8.35 us
    convert_element_type x2, other arithmetic, adam_update(): (param.astype(jnp.float32) - rate * update).astype(jnp.bfloat16)  2.76 us

profile of v1, /device:TPU:0, one launch (start us, length us, event | category | flops | bytes accessed | tf_op | source)
XLA Modules:
  0.0 116.5 jit_solution(620827834695311807)
XLA Ops:
  1.3 0.0 copy-start
  1.3 1.0 copy-done
  2.3 0.0 copy-start.1
  2.3 0.8 copy-done.1
  3.2 0.0 copy-start.2
  3.2 1.6 %copy-done.2 = bf16[512,2048]{1,0:T(8,128)(2,1)S(1)} copy-done((bf16[512,2048]{1,0:T(8,128)(2,1)S(1)}, bf16[512,2048]{1,0:T(8,128)(2,1)}, u32[]{:S(2)}) %copy-start.2) | copy-done | bytes 2097176
  4.8 0.0 copy-start.3
  4.8 1.2 %copy-done.3 = bf16[2048,256]{1,0:T(8,128)(2,1)S(1)} copy-done((bf16[2048,256]{1,0:T(8,128)(2,1)S(1)}, bf16[2048,256]{1,0:T(8,128)(2,1)}, u32[]{:S(2)}) %copy-start.3) | copy-done | bytes 1048600
  6.0 0.0 copy-start.4
  6.0 0.9 copy-done.4
  6.9 0.0 copy-start.5
  6.9 0.7 copy-done.5
  7.6 0.0 copy-start.6
  7.6 0.7 copy-done.6
  8.3 0.0 copy-start.7
  8.3 0.7 copy-done.7
  8.9 0.0 copy-start.8
  8.9 0.0 copy-start.9
  8.9 104.1 %shard_map.180 = (bf16[128,1024]{1,0:T(8,128)(2,1)S(1)}, f32[2,64,2048]{2,1,0:T(8,128)S(1)}, f32[2,16,1024]{2,1,0:T(8,128)S(1)}) custom-call(s32[8]{0:T(128)S(1)} %copy-done.6, s32[1,2]{1,0:T(1,128)S(1)} %copy-done.7, s32[1]{0:T(128)S(6)} %copy.21.count_ref, s32[1,512]{1,0:T(1,128)S(1)} %bitcast.10, bf16[512,2048]{1,0:T(8,128)(2,1)S(1)} %copy-done.2, ...), custom_call_target="tpu_custom_call" | custom-call | flops 3221225472 | bytes 8388608 | tf_op jit(solution)/shard_map/pallas_call | solution.py:558
  113.0 0.0 copy-done.8
  113.0 0.0 copy-done.9
  113.0 0.0 copy-start.10
  113.0 0.0 copy-start.11
  113.0 2.0 %subtract_convert_fusion = (bf16[2,2048,64]{1,2,0:T(8,128)(2,1)}, f32[2,2048,64]{1,2,0:T(8,128)}, f32[2,2048,64]{1,2,0:T(8,128)}) fusion(bf16[2,2048,64]{1,2,0:T(8,128)(2,1)S(1)} %copy-done, f32[2,64,2048]{2,1,0:T(8,128)S(1)} %get-tuple-element.11, f32[2,2048,64]{1,2,0:T(8,128)S(1)} %copy-done.8, f32[2,2048,64]{1,2,0:T(8,128)S(1)} %copy-done.9), kind=kLoop, calls=%fused_computation.4 | loop fusion | flops 3670016 | bytes 6291456 | tf_op jit(solution)/shard_map/convert_element_type | solution.py:23
  115.0 0.0 copy-done.10
  115.0 0.0 copy-done.11
  115.0 0.8 subtract_convert_fusion.1
  115.8 0.7 copy.22
Async XLA Ops:
  1.3 1.0 copy-start
  2.3 0.8 copy-start.1
  3.2 1.6 %copy-start.2 = (bf16[512,2048]{1,0:T(8,128)(2,1)S(1)}, bf16[512,2048]{1,0:T(8,128)(2,1)}, u32[]{:S(2)}) copy-start(bf16[512,2048]{1,0:T(8,128)(2,1)} %tokens_ref.1) | copy-start | bytes 6291460
  4.8 1.2 %copy-start.3 = (bf16[2048,256]{1,0:T(8,128)(2,1)S(1)}, bf16[2048,256]{1,0:T(8,128)(2,1)}, u32[]{:S(2)}) copy-start(bf16[2048,256]{1,0:T(8,128)(2,1)} %w_ref.1) | copy-start | bytes 3145732
  6.0 0.9 copy-start.4
  6.9 0.7 copy-start.5
  7.6 0.7 copy-start.6
  8.3 0.7 copy-start.7
  8.9 104.1 %copy-start.8 = (f32[2,2048,64]{1,2,0:T(8,128)S(1)}, f32[2,2048,64]{1,2,0:T(8,128)}, u32[]{:S(2)}) copy-start(f32[2,2048,64]{1,2,0:T(8,128)} %param.20) | copy-start | bytes 3145732
  8.9 104.1 %copy-start.9 = (f32[2,2048,64]{1,2,0:T(8,128)S(1)}, f32[2,2048,64]{1,2,0:T(8,128)}, u32[]{:S(2)}) copy-start(f32[2,2048,64]{1,2,0:T(8,128)} %param.18) | copy-start | bytes 3145732
  113.0 2.0 %copy-start.10 = (f32[2,16,1024]{2,1,0:T(8,128)S(1)}, f32[2,16,1024]{2,1,0:T(8,128)}, u32[]{:S(2)}) copy-start(f32[2,16,1024]{2,1,0:T(8,128)} %param.21) | copy-start | bytes 393220
  113.0 2.0 %copy-start.11 = (f32[2,16,1024]{2,1,0:T(8,128)S(1)}, f32[2,16,1024]{2,1,0:T(8,128)}, u32[]{:S(2)}) copy-start(f32[2,16,1024]{2,1,0:T(8,128)} %param.19) | copy-start | bytes 393220

commit v2 on v1

--- a/solution.py
+++ b/solution.py
@@ -148,14 +148,17 @@
     list_ref,
     count_ref,
     token_slot_ref,
-    tokens_ref,
+    tokens_in,
     cot_ref,
     w_ref,
-    a_ref,
-    b_ref,
+    a_in,
+    b_in,
     out_ref,
     total_a_ref,
     total_b_ref,
+    tokens_ref,
+    a_ref,
+    b_ref,
     info,
     cot_all,
     w_all,
@@ -187,6 +190,7 @@
     wg_recv_sem,
     part_send_sem,
     part_recv_sem,
+    local_sem,
 ):
     me = lax.axis_index("node")
     chip = lax.axis_index("chip")
@@ -199,6 +203,20 @@
     w_cols = w_ref.shape[1]
     half = depth // groups
 
+    loads = [
+        pltpu.make_async_copy(src, dst, local_sem.at[i])
+        for i, (src, dst) in enumerate(
+            (
+                (b_in, b_ref),
+                (a_in, a_ref),
+                (cot_ref, cot_all.at[rows_of(chip, out_rows)]),
+                (tokens_in, tokens_ref),
+                (w_ref, w_all.at[me]),
+            )
+        )
+    ]
+    for load in loads:
+        load.start()
     barrier = pltpu.get_barrier_semaphore()
     for axis, size, here in (("node", nodes, me), ("chip", chips, chip), ("groups", groups, group)):
         for o in range(1, size):
@@ -318,8 +336,9 @@
 
     w_send(0, 0)
     w_send(1, 0)
-    cot_all[rows_of(chip, out_rows), :] = cot_ref[...]
-
+
+    loads[0].wait()
+    loads[1].wait()
     landed(info_copies)
 
     def picks(q):
@@ -358,6 +377,7 @@
         else:
             recv_a[rows_of(me, rank), :] = chosen
 
+    loads[2].wait()
     landed(cot_copies)
     landed(b_copies)
     every = lax.dot_general(recv_b[...], cot_all[...], NT, preferred_element_type=F32)
@@ -379,6 +399,7 @@
 
     whole_back = back_all[...].astype(F32)
     spread_back = jnp.concatenate([masks[p] * whole_back for p in range(nodes)], axis=0).astype(BF16)
+    loads[3].wait()
     tile = min(512, depth)
     for t in range(depth // tile):
         cols = slice(t * tile, (t + 1) * tile)
@@ -388,11 +409,10 @@
     ga_copies = exchange(
         "node", nodes, me, ga_sem, lambda q: grad_a.at[rows_of(q, rank)], got_a.at[rows_of(me, rank)]
     )
-    start(ga_copies)
     got_a[rows_of(me, rank), :] = grad_a[rows_of(me, rank), :]
-
     if nodes > 2:
         w_step(1)
+    start(ga_copies)
 
     landed(a_copies)
     low_all[...] = lax.dot_general(
@@ -460,7 +480,8 @@
         lax.fori_loop(0, chips, body, 0)
         start(part_copies(shard))
 
-    chunk(me, w_ref)
+    loads[4].wait()
+    chunk(me, w_all.at[me])
     for j in range(nodes - 1):
         if j >= 2:
             w_step(j)
@@ -562,9 +583,12 @@
             jax.ShapeDtypeStruct((owned, rank, depth), F32),
             jax.ShapeDtypeStruct((owned, rank_part, width), F32),
         ),
-        in_specs=[smem] * 3 + [vmem] * 6,
+        in_specs=[smem] * 3 + [vmem] + [pl.BlockSpec(memory_space=pl.ANY)] * 5,
         out_specs=(vmem, vmem, vmem),
         scratch_shapes=[
+            pltpu.VMEM((rows, depth), BF16),
+            pltpu.VMEM((owned, rank, depth), BF16),
+            pltpu.VMEM((owned, rank_part, width), BF16),
             pltpu.VMEM((nodes, 8, 128), jnp.int32),
             pltpu.VMEM((rows, width), BF16),
             pltpu.VMEM((nodes, depth, w_cols), BF16),
@@ -596,9 +620,10 @@
             dma((2, nodes - 1, groups - 1)),
             dma((nodes, chips - 1)),
             dma((nodes, chips - 1)),
+            dma((5,)),
         ],
         compiler_params=pltpu.CompilerParams(
-            collective_id=0, has_side_effects=True, vmem_limit_bytes=48 * 1024 * 1024
+            collective_id=0, has_side_effects=True, vmem_limit_bytes=60 * 1024 * 1024
         ),
         cost_estimate=pl.CostEstimate(
             flops=2 * rows * depth * (width + 2 * nodes * rank),

time: 117 us -> 111 us (0.949)
  local copies, waits for them, and re-layouts: 8.35 us -> 0.74 us
  other arithmetic: 2.76 us -> 4.08 us
    unnamed x25 -> x17, local copies, waits for them, and re-layouts: 8.35 us -> 0.74 us
    convert_element_type x2, other arithmetic: 2.76 us -> 4.08 us  [adam_update(): (param.astype(jnp.float32) - rate * update).astype(jnp.bfloat16)]
where the time goes in v2:
time: 111 us
  Pallas kernels  105 us (95%)
  other arithmetic  4.08 us (4%)
  between operations  1.39 us (1%)
    pallas_call x1, Pallas kernels, local_fused(): pl.pallas_call(functools.partial(step_kernel, nodes, chips, groups), out_...  105 us
    convert_element_type x2, other arithmetic, adam_update(): (param.astype(jnp.float32) - rate * update).astype(jnp.bfloat16)  4.08 us

profile of v2, /device:TPU:0, one launch (start us, length us, event | category | flops | bytes accessed | tf_op | source)
XLA Modules:
  0.0 111.1 jit_solution(9478168384366005211)
XLA Ops:
  1.3 0.0 copy-start
  1.3 0.0 copy-start.1
  1.3 0.0 copy-start.2
  1.3 104.8 %shard_map.180 = (bf16[128,1024]{1,0:T(8,128)(2,1)}, f32[2,64,2048]{2,1,0:T(8,128)}, f32[2,16,1024]{2,1,0:T(8,128)}) custom-call(s32[8]{0:T(128)} %slot_ref.1, s32[1,2]{1,0:T(1,128)} %list_ref.1, s32[1]{0:T(128)S(6)} %copy.21.count_ref, s32[1,512]{1,0:T(1,128)} %bitcast.10, bf16[512,2048]{1,0:T(8,128)(2,1)} %tokens_in.1, bf16[128,1024]{1,0:T(8,128)(2,1)} %cot_ref.1, ...), custom_call_target="tpu_custom_call" | custom-call | flops 3221225472 | bytes 8388608 | tf_op jit(solution)/shard_map/pallas_call | solution.py:579
  106.2 0.0 copy-done
  106.2 0.0 copy-done.1
  106.2 0.0 copy-done.2
  106.2 0.0 copy-start.4
  106.2 0.0 copy-start.5
  106.2 0.0 copy-start.6
  106.2 0.0 copy-start.7
  106.2 0.0 copy-start.3
  106.3 3.3 %subtract_convert_fusion = (bf16[2,2048,64]{1,2,0:T(8,128)(2,1)}, f32[2,2048,64]{1,2,0:T(8,128)}, f32[2,2048,64]{1,2,0:T(8,128)}) fusion(bf16[2,2048,64]{1,2,0:T(8,128)(2,1)S(1)} %copy-done.2, f32[2,64,2048]{2,1,0:T(8,128)} %get-tuple-element.11, f32[2,2048,64]{1,2,0:T(8,128)S(1)} %copy-done, f32[2,2048,64]{1,2,0:T(8,128)S(1)} %copy-done.1), kind=kLoop, calls=%fused_computation.4 | loop fusion | flops 3670016 | bytes 6291456 | tf_op jit(solution)/shard_map/convert_element_type | solution.py:23
  109.6 0.0 copy-done.4
  109.6 0.0 copy-done.5
  109.6 0.0 copy-done.6
  109.6 0.0 copy-done.7
  109.6 0.8 subtract_convert_fusion.1
  110.4 0.0 copy-done.3
  110.4 0.7 copy.22
Async XLA Ops:
  1.3 104.9 %copy-start = (f32[2,2048,64]{1,2,0:T(8,128)S(1)}, f32[2,2048,64]{1,2,0:T(8,128)}, u32[]{:S(2)}) copy-start(f32[2,2048,64]{1,2,0:T(8,128)} %param.20) | copy-start | bytes 3145732
  1.3 104.9 %copy-start.1 = (f32[2,2048,64]{1,2,0:T(8,128)S(1)}, f32[2,2048,64]{1,2,0:T(8,128)}, u32[]{:S(2)}) copy-start(f32[2,2048,64]{1,2,0:T(8,128)} %param.18) | copy-start | bytes 3145732
  1.3 104.9 %copy-start.2 = (bf16[2,2048,64]{1,2,0:T(8,128)(2,1)S(1)}, bf16[2,2048,64]{1,2,0:T(8,128)(2,1)}, u32[]{:S(2)}) copy-start(bf16[2,2048,64]{1,2,0:T(8,128)(2,1)} %param.16) | copy-start | bytes 1572868
  106.2 3.4 %copy-start.4 = (f32[2,16,1024]{2,1,0:T(8,128)S(1)}, f32[2,16,1024]{2,1,0:T(8,128)}, u32[]{:S(2)}) copy-start(f32[2,16,1024]{2,1,0:T(8,128)} %param.21) | copy-start | bytes 393220
  106.2 3.4 %copy-start.5 = (f32[2,16,1024]{2,1,0:T(8,128)S(1)}, f32[2,16,1024]{2,1,0:T(8,128)}, u32[]{:S(2)}) copy-start(f32[2,16,1024]{2,1,0:T(8,128)} %param.19) | copy-start | bytes 393220
  106.2 3.4 %copy-start.6 = (f32[2,16,1024]{2,1,0:T(8,128)S(1)}, f32[2,16,1024]{2,1,0:T(8,128)}, u32[]{:S(2)}) copy-start(f32[2,16,1024]{2,1,0:T(8,128)} %get-tuple-element.12) | copy-start | bytes 393220
  106.2 3.4 %copy-start.7 = (bf16[2,16,1024]{2,1,0:T(8,128)(2,1)S(1)}, bf16[2,16,1024]{2,1,0:T(8,128)(2,1)}, u32[]{:S(2)}) copy-start(bf16[2,16,1024]{2,1,0:T(8,128)(2,1)} %b_in.1) | copy-start | bytes 196612
  106.2 4.1 %copy-start.3 = (bf16[128,1024]{1,0:T(8,128)(2,1)S(1)}, bf16[128,1024]{1,0:T(8,128)(2,1)}, u32[]{:S(2)}) copy-start(bf16[128,1024]{1,0:T(8,128)(2,1)} %get-tuple-element.26) | copy-start | bytes 786436

commit v3 on v2

--- a/solution.py
+++ b/solution.py
@@ -412,7 +412,6 @@
     got_a[rows_of(me, rank), :] = grad_a[rows_of(me, rank), :]
     if nodes > 2:
         w_step(1)
-    start(ga_copies)
 
     landed(a_copies)
     low_all[...] = lax.dot_general(
@@ -485,6 +484,8 @@
     for j in range(nodes - 1):
         if j >= 2:
             w_step(j)
+        if j == nodes - 2:
+            start(ga_copies)
         for way in (0, 1):
             have, shard = w_from(way, j)
 

time: 111 us -> 100 us (0.901)
  the two profiles are of different devices: /device:TPU:0 before, /device:TPU:24 now
where the time goes in v3:
time: 100 us
  Pallas kernels  93.8 us (94%)
  other arithmetic  4.08 us (4%)
  between operations  1.39 us (1%)
    pallas_call x1, Pallas kernels, local_fused(): pl.pallas_call(functools.partial(step_kernel, nodes, chips, groups), out_...  93.8 us
    convert_element_type x2, other arithmetic, adam_update(): (param.astype(jnp.float32) - rate * update).astype(jnp.bfloat16)  4.08 us

profile of v3, /device:TPU:24, one launch (start us, length us, event | category | flops | bytes accessed | tf_op | source)
XLA Modules:
  0.0 100.0 jit_solution(3125912753995780116)
XLA Ops:
  1.3 0.0 copy-start
  1.3 0.0 copy-start.1
  1.3 0.0 copy-start.2
  1.3 93.8 %shard_map.180 = (bf16[128,1024]{1,0:T(8,128)(2,1)}, f32[2,64,2048]{2,1,0:T(8,128)}, f32[2,16,1024]{2,1,0:T(8,128)}) custom-call(s32[8]{0:T(128)} %slot_ref.1, s32[1,2]{1,0:T(1,128)} %list_ref.1, s32[1]{0:T(128)S(6)} %copy.21.count_ref, s32[1,512]{1,0:T(1,128)} %bitcast.10, bf16[512,2048]{1,0:T(8,128)(2,1)} %tokens_in.1, bf16[128,1024]{1,0:T(8,128)(2,1)} %cot_ref.1, ...), custom_call_target="tpu_custom_call" | custom-call | flops 3221225472 | bytes 8388608 | tf_op jit(solution)/shard_map/pallas_call | solution.py:580
  95.1 0.0 copy-done
  95.1 0.0 copy-done.1
  95.1 0.0 copy-done.2
  95.1 0.0 copy-start.4
  95.2 0.0 copy-start.5
  95.2 0.0 copy-start.6
  95.2 0.0 copy-start.7
  95.2 0.0 copy-start.3
  95.2 3.3 %subtract_convert_fusion = (bf16[2,2048,64]{1,2,0:T(8,128)(2,1)}, f32[2,2048,64]{1,2,0:T(8,128)}, f32[2,2048,64]{1,2,0:T(8,128)}) fusion(bf16[2,2048,64]{1,2,0:T(8,128)(2,1)S(1)} %copy-done.2, f32[2,64,2048]{2,1,0:T(8,128)} %get-tuple-element.11, f32[2,2048,64]{1,2,0:T(8,128)S(1)} %copy-done, f32[2,2048,64]{1,2,0:T(8,128)S(1)} %copy-done.1), kind=kLoop, calls=%fused_computation.4 | loop fusion | flops 3670016 | bytes 6291456 | tf_op jit(solution)/shard_map/convert_element_type | solution.py:23
  98.5 0.0 copy-done.4
  98.5 0.0 copy-done.5
  98.5 0.0 copy-done.6
  98.5 0.0 copy-done.7
  98.5 0.8 subtract_convert_fusion.1
  99.3 0.0 copy-done.3
  99.3 0.7 copy.22
Async XLA Ops:
  1.3 93.8 %copy-start = (f32[2,2048,64]{1,2,0:T(8,128)S(1)}, f32[2,2048,64]{1,2,0:T(8,128)}, u32[]{:S(2)}) copy-start(f32[2,2048,64]{1,2,0:T(8,128)} %param.20) | copy-start | bytes 3145732
  1.3 93.8 %copy-start.1 = (f32[2,2048,64]{1,2,0:T(8,128)S(1)}, f32[2,2048,64]{1,2,0:T(8,128)}, u32[]{:S(2)}) copy-start(f32[2,2048,64]{1,2,0:T(8,128)} %param.18) | copy-start | bytes 3145732
  1.3 93.8 %copy-start.2 = (bf16[2,2048,64]{1,2,0:T(8,128)(2,1)S(1)}, bf16[2,2048,64]{1,2,0:T(8,128)(2,1)}, u32[]{:S(2)}) copy-start(bf16[2,2048,64]{1,2,0:T(8,128)(2,1)} %param.16) | copy-start | bytes 1572868
  95.1 3.4 %copy-start.4 = (f32[2,16,1024]{2,1,0:T(8,128)S(1)}, f32[2,16,1024]{2,1,0:T(8,128)}, u32[]{:S(2)}) copy-start(f32[2,16,1024]{2,1,0:T(8,128)} %param.21) | copy-start | bytes 393220
  95.2 3.4 %copy-start.5 = (f32[2,16,1024]{2,1,0:T(8,128)S(1)}, f32[2,16,1024]{2,1,0:T(8,128)}, u32[]{:S(2)}) copy-start(f32[2,16,1024]{2,1,0:T(8,128)} %param.19) | copy-start | bytes 393220
  95.2 3.4 %copy-start.6 = (f32[2,16,1024]{2,1,0:T(8,128)S(1)}, f32[2,16,1024]{2,1,0:T(8,128)}, u32[]{:S(2)}) copy-start(f32[2,16,1024]{2,1,0:T(8,128)} %get-tuple-element.12) | copy-start | bytes 393220
  95.2 3.4 %copy-start.7 = (bf16[2,16,1024]{2,1,0:T(8,128)(2,1)S(1)}, bf16[2,16,1024]{2,1,0:T(8,128)(2,1)}, u32[]{:S(2)}) copy-start(bf16[2,16,1024]{2,1,0:T(8,128)(2,1)} %b_in.1) | copy-start | bytes 196612
  95.2 4.1 %copy-start.3 = (bf16[128,1024]{1,0:T(8,128)(2,1)S(1)}, bf16[128,1024]{1,0:T(8,128)(2,1)}, u32[]{:S(2)}) copy-start(bf16[128,1024]{1,0:T(8,128)(2,1)} %get-tuple-element.26) | copy-start | bytes 786436

commit v4 on v2

--- a/solution.py
+++ b/solution.py
@@ -412,7 +412,19 @@
     got_a[rows_of(me, rank), :] = grad_a[rows_of(me, rank), :]
     if nodes > 2:
         w_step(1)
-    start(ga_copies)
+
+    def start_ga(to_inner):
+        for o in range(1, nodes):
+            q = lax.rem(me + o, nodes)
+            inner = (q > 0) & (q < nodes - 1)
+
+            @pl.when(inner if to_inner else jnp.logical_not(inner))
+            def _():
+                ga_copies[o - 1].start()
+
+    start_ga(True)
+    if nodes <= 3:
+        start_ga(False)
 
     landed(a_copies)
     low_all[...] = lax.dot_general(
@@ -483,8 +495,10 @@
     loads[4].wait()
     chunk(me, w_all.at[me])
     for j in range(nodes - 1):
-        if j >= 2:
-            w_step(j)
+        if 1 <= j < nodes - 2:
+            w_step(j + 1)
+            if j + 1 == nodes - 2:
+                start_ga(False)
         for way in (0, 1):
             have, shard = w_from(way, j)
 

time: 111 us -> 110 us (level)
  no operation moved by 1% of the time
where the time goes in v4:
time: 110 us
  Pallas kernels  104 us (95%)
  other arithmetic  4.08 us (4%)
  between operations  1.39 us (1%)
    pallas_call x1, Pallas kernels, local_fused(): pl.pallas_call(functools.partial(step_kernel, nodes, chips, groups), out_...  104 us
    convert_element_type x2, other arithmetic, adam_update(): (param.astype(jnp.float32) - rate * update).astype(jnp.bfloat16)  4.08 us

profile of v4, /device:TPU:0, one launch (start us, length us, event | category | flops | bytes accessed | tf_op | source)
XLA Modules:
  0.0 110.2 jit_solution(1862739032234107353)
XLA Ops:
  1.3 0.0 copy-start
  1.3 0.0 copy-start.1
  1.3 0.0 copy-start.2
  1.3 104.0 %shard_map.180 = (bf16[128,1024]{1,0:T(8,128)(2,1)}, f32[2,64,2048]{2,1,0:T(8,128)}, f32[2,16,1024]{2,1,0:T(8,128)}) custom-call(s32[8]{0:T(128)} %slot_ref.1, s32[1,2]{1,0:T(1,128)} %list_ref.1, s32[1]{0:T(128)S(6)} %copy.21.count_ref, s32[1,512]{1,0:T(1,128)} %bitcast.10, bf16[512,2048]{1,0:T(8,128)(2,1)} %tokens_in.1, bf16[128,1024]{1,0:T(8,128)(2,1)} %cot_ref.1, ...), custom_call_target="tpu_custom_call" | custom-call | flops 3221225472 | bytes 8388608 | tf_op jit(solution)/shard_map/pallas_call | solution.py:593
  105.3 0.0 copy-done
  105.3 0.0 copy-done.1
  105.4 0.0 copy-done.2
  105.4 0.0 copy-start.4
  105.4 0.0 copy-start.5
  105.4 0.0 copy-start.6
  105.4 0.0 copy-start.7
  105.4 0.0 copy-start.3
  105.4 3.3 %subtract_convert_fusion = (bf16[2,2048,64]{1,2,0:T(8,128)(2,1)}, f32[2,2048,64]{1,2,0:T(8,128)}, f32[2,2048,64]{1,2,0:T(8,128)}) fusion(bf16[2,2048,64]{1,2,0:T(8,128)(2,1)S(1)} %copy-done.2, f32[2,64,2048]{2,1,0:T(8,128)} %get-tuple-element.11, f32[2,2048,64]{1,2,0:T(8,128)S(1)} %copy-done, f32[2,2048,64]{1,2,0:T(8,128)S(1)} %copy-done.1), kind=kLoop, calls=%fused_computation.4 | loop fusion | flops 3670016 | bytes 6291456 | tf_op jit(solution)/shard_map/convert_element_type | solution.py:23
  108.7 0.0 copy-done.4
  108.7 0.0 copy-done.5
  108.7 0.0 copy-done.6
  108.7 0.0 copy-done.7
  108.8 0.8 subtract_convert_fusion.1
  109.5 0.0 copy-done.3
  109.5 0.7 copy.22
Async XLA Ops:
  1.3 104.1 %copy-start = (f32[2,2048,64]{1,2,0:T(8,128)S(1)}, f32[2,2048,64]{1,2,0:T(8,128)}, u32[]{:S(2)}) copy-start(f32[2,2048,64]{1,2,0:T(8,128)} %param.20) | copy-start | bytes 3145732
  1.3 104.1 %copy-start.1 = (f32[2,2048,64]{1,2,0:T(8,128)S(1)}, f32[2,2048,64]{1,2,0:T(8,128)}, u32[]{:S(2)}) copy-start(f32[2,2048,64]{1,2,0:T(8,128)} %param.18) | copy-start | bytes 3145732
  1.3 104.1 %copy-start.2 = (bf16[2,2048,64]{1,2,0:T(8,128)(2,1)S(1)}, bf16[2,2048,64]{1,2,0:T(8,128)(2,1)}, u32[]{:S(2)}) copy-start(bf16[2,2048,64]{1,2,0:T(8,128)(2,1)} %param.16) | copy-start | bytes 1572868
  105.4 3.4 %copy-start.4 = (f32[2,16,1024]{2,1,0:T(8,128)S(1)}, f32[2,16,1024]{2,1,0:T(8,128)}, u32[]{:S(2)}) copy-start(f32[2,16,1024]{2,1,0:T(8,128)} %param.21) | copy-start | bytes 393220
  105.4 3.4 %copy-start.5 = (f32[2,16,1024]{2,1,0:T(8,128)S(1)}, f32[2,16,1024]{2,1,0:T(8,128)}, u32[]{:S(2)}) copy-start(f32[2,16,1024]{2,1,0:T(8,128)} %param.19) | copy-start | bytes 393220
  105.4 3.4 %copy-start.6 = (f32[2,16,1024]{2,1,0:T(8,128)S(1)}, f32[2,16,1024]{2,1,0:T(8,128)}, u32[]{:S(2)}) copy-start(f32[2,16,1024]{2,1,0:T(8,128)} %get-tuple-element.12) | copy-start | bytes 393220
  105.4 3.4 %copy-start.7 = (bf16[2,16,1024]{2,1,0:T(8,128)(2,1)S(1)}, bf16[2,16,1024]{2,1,0:T(8,128)(2,1)}, u32[]{:S(2)}) copy-start(bf16[2,16,1024]{2,1,0:T(8,128)(2,1)} %b_in.1) | copy-start | bytes 196612
  105.4 4.1 %copy-start.3 = (bf16[128,1024]{1,0:T(8,128)(2,1)S(1)}, bf16[128,1024]{1,0:T(8,128)(2,1)}, u32[]{:S(2)}) copy-start(bf16[128,1024]{1,0:T(8,128)(2,1)} %get-tuple-element.26) | copy-start | bytes 786436

commit v5 on v3

--- a/solution.py
+++ b/solution.py
@@ -373,7 +373,6 @@
         chosen = sum(pick[j] * a_ref[j].astype(F32) for j in range(owned)).astype(BF16)
         if o < nodes:
             send_a[rows_of(q, rank), :] = chosen
-            a_copies[o - 1].start()
         else:
             recv_a[rows_of(me, rank), :] = chosen
 
@@ -395,6 +394,7 @@
     )
     start(back_copies)
     w_step(0)
+    start(a_copies)
     landed(back_copies)
 
     whole_back = back_all[...].astype(F32)

time: 100 us -> 97.6 us (0.976)
  the two profiles are of different devices: /device:TPU:24 before, /device:TPU:25 now
where the time goes in v5:
time: 97.6 us; the launch traced here: 97.4 us
  Pallas kernels  91.2 us (93%)
  other arithmetic  4.08 us (4%)
  between operations  1.39 us (1%)
    pallas_call x1, Pallas kernels, local_fused(): pl.pallas_call(functools.partial(step_kernel, nodes, chips, groups), out_...  91.2 us
    convert_element_type x2, other arithmetic, adam_update(): (param.astype(jnp.float32) - rate * update).astype(jnp.bfloat16)  4.08 us

profile of v5, /device:TPU:25, one launch (start us, length us, event | category | flops | bytes accessed | tf_op | source)
XLA Modules:
  0.0 97.4 jit_solution(15636417521904307211)
XLA Ops:
  1.3 0.0 copy-start
  1.3 0.0 copy-start.1
  1.3 0.0 copy-start.2
  1.3 91.2 %shard_map.180 = (bf16[128,1024]{1,0:T(8,128)(2,1)}, f32[2,64,2048]{2,1,0:T(8,128)}, f32[2,16,1024]{2,1,0:T(8,128)}) custom-call(s32[8]{0:T(128)} %slot_ref.1, s32[1,2]{1,0:T(1,128)} %list_ref.1, s32[1]{0:T(128)S(6)} %copy.21.count_ref, s32[1,512]{1,0:T(1,128)} %bitcast.10, bf16[512,2048]{1,0:T(8,128)(2,1)} %tokens_in.1, bf16[128,1024]{1,0:T(8,128)(2,1)} %cot_ref.1, ...), custom_call_target="tpu_custom_call" | custom-call | flops 3221225472 | bytes 8388608 | tf_op jit(solution)/shard_map/pallas_call | solution.py:580
  92.5 0.0 copy-done
  92.6 0.0 copy-done.1
  92.6 0.0 copy-done.2
  92.6 0.0 copy-start.4
  92.6 0.0 copy-start.5
  92.6 0.0 copy-start.6
  92.6 0.0 copy-start.7
  92.6 0.0 copy-start.3
  92.6 3.3 %subtract_convert_fusion = (bf16[2,2048,64]{1,2,0:T(8,128)(2,1)}, f32[2,2048,64]{1,2,0:T(8,128)}, f32[2,2048,64]{1,2,0:T(8,128)}) fusion(bf16[2,2048,64]{1,2,0:T(8,128)(2,1)S(1)} %copy-done.2, f32[2,64,2048]{2,1,0:T(8,128)} %get-tuple-element.11, f32[2,2048,64]{1,2,0:T(8,128)S(1)} %copy-done, f32[2,2048,64]{1,2,0:T(8,128)S(1)} %copy-done.1), kind=kLoop, calls=%fused_computation.4 | loop fusion | flops 3670016 | bytes 6291456 | tf_op jit(solution)/shard_map/convert_element_type | solution.py:23
  96.0 0.0 copy-done.4
  96.0 0.0 copy-done.5
  96.0 0.0 copy-done.6
  96.0 0.0 copy-done.7
  96.0 0.8 subtract_convert_fusion.1
  96.7 0.0 copy-done.3
  96.7 0.7 copy.22
Async XLA Ops:
  1.3 91.3 %copy-start = (f32[2,2048,64]{1,2,0:T(8,128)S(1)}, f32[2,2048,64]{1,2,0:T(8,128)}, u32[]{:S(2)}) copy-start(f32[2,2048,64]{1,2,0:T(8,128)} %param.20) | copy-start | bytes 3145732
  1.3 91.3 %copy-start.1 = (f32[2,2048,64]{1,2,0:T(8,128)S(1)}, f32[2,2048,64]{1,2,0:T(8,128)}, u32[]{:S(2)}) copy-start(f32[2,2048,64]{1,2,0:T(8,128)} %param.18) | copy-start | bytes 3145732
  1.3 91.3 %copy-start.2 = (bf16[2,2048,64]{1,2,0:T(8,128)(2,1)S(1)}, bf16[2,2048,64]{1,2,0:T(8,128)(2,1)}, u32[]{:S(2)}) copy-start(bf16[2,2048,64]{1,2,0:T(8,128)(2,1)} %param.16) | copy-start | bytes 1572868
  92.6 3.4 %copy-start.4 = (f32[2,16,1024]{2,1,0:T(8,128)S(1)}, f32[2,16,1024]{2,1,0:T(8,128)}, u32[]{:S(2)}) copy-start(f32[2,16,1024]{2,1,0:T(8,128)} %param.21) | copy-start | bytes 393220
  92.6 3.4 %copy-start.5 = (f32[2,16,1024]{2,1,0:T(8,128)S(1)}, f32[2,16,1024]{2,1,0:T(8,128)}, u32[]{:S(2)}) copy-start(f32[2,16,1024]{2,1,0:T(8,128)} %param.19) | copy-start | bytes 393220
  92.6 3.4 %copy-start.6 = (f32[2,16,1024]{2,1,0:T(8,128)S(1)}, f32[2,16,1024]{2,1,0:T(8,128)}, u32[]{:S(2)}) copy-start(f32[2,16,1024]{2,1,0:T(8,128)} %get-tuple-element.12) | copy-start | bytes 393220
  92.6 3.4 %copy-start.7 = (bf16[2,16,1024]{2,1,0:T(8,128)(2,1)S(1)}, bf16[2,16,1024]{2,1,0:T(8,128)(2,1)}, u32[]{:S(2)}) copy-start(bf16[2,16,1024]{2,1,0:T(8,128)(2,1)} %b_in.1) | copy-start | bytes 196612
  92.6 4.1 %copy-start.3 = (bf16[128,1024]{1,0:T(8,128)(2,1)S(1)}, bf16[128,1024]{1,0:T(8,128)(2,1)}, u32[]{:S(2)}) copy-start(bf16[128,1024]{1,0:T(8,128)(2,1)} %get-tuple-element.26) | copy-start | bytes 786436
